TPU v7x, 32 devices: a whole 2x2x4 slice. The times are simulated.
32 devices in a mesh: row: 8 (over z, x), col: 4 (over y, core).
Axes of the slice: x: 2, y: 2, z: 4, core: 2. Of those that a mesh axis runs over, the one named last changes fastest.
Arguments:
- blocks: bfloat16 [256, 16, 128, 128], P('row', 'col'), may hold values from -0.375 to 0.375
- pattern: int32 [256, 16], replicated, may hold values from 0 to 255, as said below
- owners: int32 [4, 256, 4, 1], P('col', 'row'), may hold values from 0 to 7; in each aligned block of 128 rows (0 to 127, 128 to 255, ..., all dimensions but the last counted through in order) at most 24 rows name the same one
Outputs:
- moved: bfloat16 [4, 8, 192, 128, 128], P('col', 'row')
Inputs may be any that keep to these rules, and one draw needn't show every extreme that they name: `pattern`: block row i holds 16 distinct column blocks (i + d) mod 256, by rising d with |d| <= 8, d = 0 among them, in slot order. `owners`: among the 128 entries of one device no value occurs more than 24 times; in some device some value occurs exactly 24 times.
All inputs are finite; a program needn't handle non-finite values.
Results may differ from a plain program's by a relative error of at most 0.0049.
Values may be sent and summed in bfloat16 or wider, within the bound.
A program may use at most 192 MiB of HBM per device.

v0:
```python
import math

import jax
import jax.numpy as jnp
from jax import lax
from jax.sharding import PartitionSpec as P


def passed_along(shard, axis, by):
    devices = lax.axis_size(axis)
    return lax.ppermute(shard, axis, [(i, (i + by) % devices) for i in range(devices)])


def local_index(pattern, start_row, row_count, margin):
    nblk, slot_count = pattern.shape
    reach = slot_count // 2
    own_cols = lax.dynamic_slice_in_dim(pattern, start_row, row_count, 0)
    row_ids = start_row + jnp.arange(row_count, dtype=jnp.int32)
    offsets = (own_cols - row_ids[:, None] + reach + nblk) % nblk - reach
    ext_row = jnp.arange(row_count, dtype=jnp.int32)[:, None] + margin + offsets
    neighbour_cols = pattern[own_cols]
    same_col = neighbour_cols[:, None, :, :] == own_cols[:, :, None, None]
    has_match = jnp.any(same_col, axis=-1)
    match_slot = jnp.sum(
        same_col.astype(jnp.int32) * jnp.arange(slot_count, dtype=jnp.int32), axis=-1
    )
    extent = (row_count + 2 * margin) * slot_count
    return jnp.where(has_match, ext_row[:, None, :] * slot_count + match_slot, extent)


def multiply(left, extended, pick_index):
    row_count, slot_count, tile_size = (left.shape[0], left.shape[1], left.shape[-1])
    target_count = pick_index.shape[1]
    group_rows = math.gcd(row_count, max(1, 32 // target_count))
    flat_table = jnp.concatenate(
        [
            extended.reshape(-1, tile_size, tile_size),
            jnp.zeros((1, tile_size, tile_size), extended.dtype),
        ],
        axis=0,
    )

    def per_group(operands):
        left_rows, pick_rows = operands
        picked = flat_table[pick_rows]
        return jnp.einsum("gtab,gstbc->gsac", left_rows, picked, preferred_element_type=jnp.float32)

    result = lax.map(
        per_group,
        (
            left.reshape(row_count // group_rows, group_rows, slot_count, tile_size, tile_size),
            pick_index.reshape(row_count // group_rows, group_rows, target_count, slot_count),
        ),
    )
    return result.reshape(row_count, target_count, tile_size, tile_size)


def per_device(blocks, pattern, owners):
    row_count, slot_share, tile_size = (blocks.shape[0], blocks.shape[1], blocks.shape[-1])
    slot_count = pattern.shape[1]
    reach = slot_count // 2
    row_pos = lax.axis_index("row")
    col_pos = lax.axis_index("col")
    row_devices = lax.axis_size("row")
    col_devices = lax.axis_size("col")
    row_blocks = lax.all_to_all(blocks, "col", split_axis=0, concat_axis=1, tiled=True)
    local_rows = row_blocks.shape[0]
    hop_count = -(-reach // local_rows)
    lower_list = []
    upper_list = []
    for distance in range(1, hop_count + 1):
        lower_list.append(passed_along(row_blocks, ("row", "col"), distance))
        upper_list.append(passed_along(row_blocks, ("row", "col"), -distance))
    extended = jnp.concatenate(lower_list[::-1] + [row_blocks] + upper_list, axis=0)
    margin = hop_count * local_rows
    start_row = (row_pos * col_devices + col_pos) * local_rows
    pick_index = local_index(pattern, start_row, local_rows, margin)
    squared = multiply(row_blocks, extended, pick_index).astype(jnp.bfloat16)
    cube_term = multiply(squared, extended, pick_index)
    result_rows = (3.0 * squared.astype(jnp.float32) - 2.0 * cube_term).astype(jnp.bfloat16)
    result = lax.all_to_all(result_rows, "col", split_axis=1, concat_axis=0, tiled=True)
    block_count = row_count * slot_share
    capacity = 3 * block_count // (2 * row_devices)
    flat_result = result.reshape(block_count, tile_size, tile_size)
    destination = owners.reshape(block_count)
    one_hot = (destination[:, None] == jnp.arange(row_devices, dtype=jnp.int32)[None, :]).astype(
        jnp.int32
    )
    bucket_rank = jnp.sum((jnp.cumsum(one_hot, axis=0) - 1) * one_hot, axis=1)
    bucket_slot = destination * capacity + bucket_rank
    wanted = jnp.arange(row_devices * capacity, dtype=jnp.int32)
    slot_match = bucket_slot[None, :] == wanted[:, None]
    has_source = jnp.any(slot_match, axis=1)
    source = jnp.sum(
        slot_match.astype(jnp.int32) * jnp.arange(block_count, dtype=jnp.int32)[None, :], axis=1
    )
    padded = jnp.concatenate(
        [flat_result, jnp.zeros((1, tile_size, tile_size), flat_result.dtype)], axis=0
    )
    buckets = padded[jnp.where(has_source, source, block_count)].reshape(
        row_devices, capacity, tile_size, tile_size
    )
    received = lax.all_to_all(buckets, "row", split_axis=0, concat_axis=0, tiled=True)
    return received.reshape(1, 1, row_devices * capacity, tile_size, tile_size)


def solution(mesh):
    in_specs = (P("row", "col", None, None), P(), P("col", "row", None, None))
    out_specs = P("col", "row", None, None, None)
    return jax.shard_map(
        per_device, mesh=mesh, in_specs=in_specs, out_specs=out_specs, check_vma=False
    )
```

profile of v0, /device:TPU:0, one launch (start us, length us, event | category | flops | bytes accessed | tf_op | source)
XLA Modules:
  0.0 626.0 jit_solution(2961413293863441832)
XLA Ops:
  0.0 52.7 %all_to_all.38 = bf16[32,4,128,128]{3,2,1,0:T(8,128)(2,1)S(1)} all-to-all(bf16[32,4,128,128]{3,2,1,0:T(8,128)(2,1)} %param.7), channel_id=1, replica_groups=mesh['row'=8,'col'=4] {'col'}, dimensions={0} | all-to-all | bytes 8388608 | tf_op jit(solution)/shard_map/all_to_all | solution.py:66
  69.1 37.8 %collective-permute-done = bf16[8,16,128,128]{3,2,1,0:T(8,128)(2,1)} collective-permute-done((bf16[8,16,128,128]{3,2,1,0:T(8,128)(2,1)}, bf16[8,16,128,128]{3,2,1,0:T(8,128)(2,1)}, u32[]{:S(2)}, u32[]{:S(2)}) %collective-permute-start) | collective-permute-done | bytes 4194336 | tf_op jit(solution)/shard_map/ppermute | solution.py:11
  120.0 118.7 %while.22 = (s32[]{:T(128)}, bf16[4,2,16,128,128]{3,4,2,1,0:T(8,128)(2,1)}, s32[4,2,16,16]{3,2,1,0:T(8,128)S(1)}, bf16[385,128,128]{2,1,0:T(8,128)(2,1)}, bf16[4,2,16,128,128]{4,3,2,1,0:T(8,128)(2,1)}) while((s32[]{:T(128)}, bf16[4,2,16,128,128]{3,4,2,1,0:T(8,128)(2,1)}, s32[4,2,16,16]{3,2,1,0:T(8,128)S(1)}, ...), condition=%wide.region_3.4_spmd.clone, body=%wide.region_2.3_spmd.sunk.clone | while | flops 2147486208 | bytes 53494848 | solution.py:48
  120.1 18.4 %gather_fusion = bf16[512,128,128]{2,1,0:T(8,128)(2,1)} fusion(bf16[385,128,128]{2,1,0:T(8,128)(2,1)} %get-tuple-element.209, s32[1024]{0:T(1024)S(1)} %pad_clamp_fusion.8), kind=kCustom, calls=%fused_computation.clone.1.clone | custom fusion | bytes 33556480 | tf_op jit(solution)/shard_map/while/body/eval_jaxpr/gather | solution.py:45
  138.5 11.1 %bitcast_dynamic-update-slice_fusion.6 = bf16[4,2,16,128,128]{3,4,2,1,0:T(8,128)(2,1)} fusion(bf16[4,2,16,128,128]{3,4,2,1,0:T(8,128)(2,1)} %get-tuple-element.202, s32[]{:T(128)} %get-tuple-element.201, bf16[2,16,16,128,128]{4,3,2,1,0:T(8,128)(2,1)} %bitcast.97, bf16[4,2,16,128,128]{4,3,2,1,0:T(8,128)(2,1)} %get-tuple-element.210), kind=kOutput, calls=%fused_computation.4.clone.1.clone | convolution fusion | flops 2147483648 | bytes 19923968 | tf_op jit(solution)/shard_map/while/body/eval_jaxpr/gtab,gstbc->gsac/dot_general | solution.py:46
  149.7 18.5 %gather_fusion = bf16[512,128,128]{2,1,0:T(8,128)(2,1)} fusion(bf16[385,128,128]{2,1,0:T(8,128)(2,1)} %get-tuple-element.209, s32[1024]{0:T(1024)S(1)} %pad_clamp_fusion.8), kind=kCustom, calls=%fused_computation.clone.1.clone | custom fusion | bytes 33556480 | tf_op jit(solution)/shard_map/while/body/eval_jaxpr/gather | solution.py:45
  168.2 11.1 %bitcast_dynamic-update-slice_fusion.6 = bf16[4,2,16,128,128]{3,4,2,1,0:T(8,128)(2,1)} fusion(bf16[4,2,16,128,128]{3,4,2,1,0:T(8,128)(2,1)} %get-tuple-element.202, s32[]{:T(128)} %get-tuple-element.201, bf16[2,16,16,128,128]{4,3,2,1,0:T(8,128)(2,1)} %bitcast.97, bf16[4,2,16,128,128]{4,3,2,1,0:T(8,128)(2,1)} %get-tuple-element.210), kind=kOutput, calls=%fused_computation.4.clone.1.clone | convolution fusion | flops 2147483648 | bytes 19923968 | tf_op jit(solution)/shard_map/while/body/eval_jaxpr/gtab,gstbc->gsac/dot_general | solution.py:46
  179.4 18.5 %gather_fusion = bf16[512,128,128]{2,1,0:T(8,128)(2,1)} fusion(bf16[385,128,128]{2,1,0:T(8,128)(2,1)} %get-tuple-element.209, s32[1024]{0:T(1024)S(1)} %pad_clamp_fusion.8), kind=kCustom, calls=%fused_computation.clone.1.clone | custom fusion | bytes 33556480 | tf_op jit(solution)/shard_map/while/body/eval_jaxpr/gather | solution.py:45
  197.9 11.1 %bitcast_dynamic-update-slice_fusion.6 = bf16[4,2,16,128,128]{3,4,2,1,0:T(8,128)(2,1)} fusion(bf16[4,2,16,128,128]{3,4,2,1,0:T(8,128)(2,1)} %get-tuple-element.202, s32[]{:T(128)} %get-tuple-element.201, bf16[2,16,16,128,128]{4,3,2,1,0:T(8,128)(2,1)} %bitcast.97, bf16[4,2,16,128,128]{4,3,2,1,0:T(8,128)(2,1)} %get-tuple-element.210), kind=kOutput, calls=%fused_computation.4.clone.1.clone | convolution fusion | flops 2147483648 | bytes 19923968 | tf_op jit(solution)/shard_map/while/body/eval_jaxpr/gtab,gstbc->gsac/dot_general | solution.py:46
  209.1 18.5 %gather_fusion = bf16[512,128,128]{2,1,0:T(8,128)(2,1)} fusion(bf16[385,128,128]{2,1,0:T(8,128)(2,1)} %get-tuple-element.209, s32[1024]{0:T(1024)S(1)} %pad_clamp_fusion.8), kind=kCustom, calls=%fused_computation.clone.1.clone | custom fusion | bytes 33556480 | tf_op jit(solution)/shard_map/while/body/eval_jaxpr/gather | solution.py:45
  227.6 11.1 %bitcast_dynamic-update-slice_fusion.6 = bf16[4,2,16,128,128]{3,4,2,1,0:T(8,128)(2,1)} fusion(bf16[4,2,16,128,128]{3,4,2,1,0:T(8,128)(2,1)} %get-tuple-element.202, s32[]{:T(128)} %get-tuple-element.201, bf16[2,16,16,128,128]{4,3,2,1,0:T(8,128)(2,1)} %bitcast.97, bf16[4,2,16,128,128]{4,3,2,1,0:T(8,128)(2,1)} %get-tuple-element.210), kind=kOutput, calls=%fused_computation.4.clone.1.clone | convolution fusion | flops 2147483648 | bytes 19923968 | tf_op jit(solution)/shard_map/while/body/eval_jaxpr/gtab,gstbc->gsac/dot_general | solution.py:46
  238.7 119.4 %while.23 = (s32[]{:T(128)}, f32[4,2,16,128,128]{3,4,2,1,0:T(8,128)}, s32[4,2,16,16]{3,2,1,0:T(8,128)S(1)}, bf16[385,128,128]{2,1,0:T(8,128)(2,1)}, bf16[4,2,16,128,128]{3,4,2,1,0:T(8,128)(2,1)}) while((s32[]{:T(128)}, f32[4,2,16,128,128]{3,4,2,1,0:T(8,128)}, s32[4,2,16,16]{3,2,1,0:T(8,128)S(1)}, bf16[385,128,128]{2,1,0:T(8,128)(2,1)}, ...), condition=%wide.region_5.6_spmd.clone, body=%wide.region_4.5_spmd.sunk.clone | while | flops 2147486208 | bytes 53494848 | solution.py:48
  238.8 18.4 %gather_fusion.1 = bf16[512,128,128]{2,1,0:T(8,128)(2,1)} fusion(bf16[385,128,128]{2,1,0:T(8,128)(2,1)} %get-tuple-element.224, s32[1024]{0:T(1024)S(1)} %pad_clamp_fusion.9), kind=kCustom, calls=%fused_computation.1.clone.1.clone | custom fusion | bytes 33556480 | tf_op jit(solution)/shard_map/while/body/eval_jaxpr/gather | solution.py:45
  257.3 11.3 %bitcast_dynamic-update-slice_fusion.7 = f32[4,2,16,128,128]{3,4,2,1,0:T(8,128)} fusion(f32[4,2,16,128,128]{3,4,2,1,0:T(8,128)} %get-tuple-element.217, s32[]{:T(128)} %get-tuple-element.216, bf16[2,16,16,128,128]{4,3,2,1,0:T(8,128)(2,1)} %bitcast.98, bf16[4,2,16,128,128]{3,4,2,1,0:T(8,128)(2,1)} %get-tuple-element.225), kind=kOutput, calls=%fused_computation.10.clone.1.clone | convolution fusion | flops 2147483648 | bytes 19923968 | tf_op jit(solution)/shard_map/while/body/eval_jaxpr/gtab,gstbc->gsac/dot_general | solution.py:46
  268.7 18.5 %gather_fusion.1 = bf16[512,128,128]{2,1,0:T(8,128)(2,1)} fusion(bf16[385,128,128]{2,1,0:T(8,128)(2,1)} %get-tuple-element.224, s32[1024]{0:T(1024)S(1)} %pad_clamp_fusion.9), kind=kCustom, calls=%fused_computation.1.clone.1.clone | custom fusion | bytes 33556480 | tf_op jit(solution)/shard_map/while/body/eval_jaxpr/gather | solution.py:45
  287.1 11.3 %bitcast_dynamic-update-slice_fusion.7 = f32[4,2,16,128,128]{3,4,2,1,0:T(8,128)} fusion(f32[4,2,16,128,128]{3,4,2,1,0:T(8,128)} %get-tuple-element.217, s32[]{:T(128)} %get-tuple-element.216, bf16[2,16,16,128,128]{4,3,2,1,0:T(8,128)(2,1)} %bitcast.98, bf16[4,2,16,128,128]{3,4,2,1,0:T(8,128)(2,1)} %get-tuple-element.225), kind=kOutput, calls=%fused_computation.10.clone.1.clone | convolution fusion | flops 2147483648 | bytes 19923968 | tf_op jit(solution)/shard_map/while/body/eval_jaxpr/gtab,gstbc->gsac/dot_general | solution.py:46
  298.5 18.5 %gather_fusion.1 = bf16[512,128,128]{2,1,0:T(8,128)(2,1)} fusion(bf16[385,128,128]{2,1,0:T(8,128)(2,1)} %get-tuple-element.224, s32[1024]{0:T(1024)S(1)} %pad_clamp_fusion.9), kind=kCustom, calls=%fused_computation.1.clone.1.clone | custom fusion | bytes 33556480 | tf_op jit(solution)/shard_map/while/body/eval_jaxpr/gather | solution.py:45
  317.0 11.3 %bitcast_dynamic-update-slice_fusion.7 = f32[4,2,16,128,128]{3,4,2,1,0:T(8,128)} fusion(f32[4,2,16,128,128]{3,4,2,1,0:T(8,128)} %get-tuple-element.217, s32[]{:T(128)} %get-tuple-element.216, bf16[2,16,16,128,128]{4,3,2,1,0:T(8,128)(2,1)} %bitcast.98, bf16[4,2,16,128,128]{3,4,2,1,0:T(8,128)(2,1)} %get-tuple-element.225), kind=kOutput, calls=%fused_computation.10.clone.1.clone | convolution fusion | flops 2147483648 | bytes 19923968 | tf_op jit(solution)/shard_map/while/body/eval_jaxpr/gtab,gstbc->gsac/dot_general | solution.py:46
  328.4 18.5 %gather_fusion.1 = bf16[512,128,128]{2,1,0:T(8,128)(2,1)} fusion(bf16[385,128,128]{2,1,0:T(8,128)(2,1)} %get-tuple-element.224, s32[1024]{0:T(1024)S(1)} %pad_clamp_fusion.9), kind=kCustom, calls=%fused_computation.1.clone.1.clone | custom fusion | bytes 33556480 | tf_op jit(solution)/shard_map/while/body/eval_jaxpr/gather | solution.py:45
  346.8 11.3 %bitcast_dynamic-update-slice_fusion.7 = f32[4,2,16,128,128]{3,4,2,1,0:T(8,128)} fusion(f32[4,2,16,128,128]{3,4,2,1,0:T(8,128)} %get-tuple-element.217, s32[]{:T(128)} %get-tuple-element.216, bf16[2,16,16,128,128]{4,3,2,1,0:T(8,128)(2,1)} %bitcast.98, bf16[4,2,16,128,128]{3,4,2,1,0:T(8,128)(2,1)} %get-tuple-element.225), kind=kOutput, calls=%fused_computation.10.clone.1.clone | convolution fusion | flops 2147483648 | bytes 19923968 | tf_op jit(solution)/shard_map/while/body/eval_jaxpr/gtab,gstbc->gsac/dot_general | solution.py:46
  373.3 42.9 %all-to-all-start.1 = ((bf16[8,16,128,128]{3,2,0,1:T(8,128)(2,1)}), bf16[8,16,128,128]{3,2,0,1:T(8,128)(2,1)}, u32[]{:S(2)}, u32[]{:S(2)}) async-start(bf16[8,16,128,128]{3,2,0,1:T(8,128)(2,1)} %bitcast.102), calls=%async_computation.1 | async-start | bytes 8388608 | tf_op jit(solution)/shard_map/all_to_all | solution.py:81
  417.1 47.3 %all-to-all-done.1 = bf16[8,16,128,128]{3,2,0,1:T(8,128)(2,1)} async-done(((bf16[8,16,128,128]{3,2,0,1:T(8,128)(2,1)}), bf16[8,16,128,128]{3,2,0,1:T(8,128)(2,1)}, u32[]{:S(2)}, u32[]{:S(2)}) %all-to-all-start.1) | async-done | bytes 4194336 | tf_op jit(solution)/shard_map/all_to_all | solution.py:81
  469.7 10.2 %gather_fusion.3 = bf16[192,128,128]{2,1,0:T(8,128)(2,1)} fusion(bf16[129,128,128]{2,1,0:T(8,128)(2,1)} %concatenate.12, s32[1024]{0:T(1024)S(1)} %pad_clamp_fusion.2), kind=kCustom, calls=%fused_computation.3 | custom fusion | bytes 12583680 | tf_op jit(solution)/shard_map/gather | solution.py:100
  479.9 143.3 %all_to_all.39 = bf16[8,24,128,128]{3,2,1,0:T(8,128)(2,1)S(1)} all-to-all(bf16[8,24,128,128]{3,2,1,0:T(8,128)(2,1)} %bitcast.100), channel_id=1, replica_groups=mesh['row'=8,'col'=4] {'row'}, dimensions={0} | all-to-all | bytes 12582912 | tf_op jit(solution)/shard_map/all_to_all | solution.py:103
  (62 shorter events, 54.3 us)
Async XLA Ops:
  0.0 60.3 %copy-start = (s32[256,16]{0,1:T(8,128)S(1)}, s32[256,16]{0,1:T(8,128)}, u32[]{:S(2)}) copy-start(s32[256,16]{0,1:T(8,128)} %param.8) | copy-start | bytes 49156
  55.0 51.9 %collective-permute-start = (bf16[8,16,128,128]{3,2,1,0:T(8,128)(2,1)}, bf16[8,16,128,128]{3,2,1,0:T(8,128)(2,1)}, u32[]{:S(2)}, u32[]{:S(2)}) collective-permute-start(bf16[8,16,128,128]{3,2,1,0:T(8,128)(2,1)} %bitcast.24), channel_id=1, source_target_pairs={{0,1},{1,2},{2,3},{3,4},{4,5},{5,6},{6,7},{7,8},{8,9},{9,10},{10,1... | collective-permute-start | bytes 12582920 | tf_op jit(solution)/shard_map/ppermute | solution.py:11
  55.0 51.9 %collective-permute-start.1 = (bf16[8,16,128,128]{3,2,1,0:T(8,128)(2,1)}, bf16[8,16,128,128]{3,2,1,0:T(8,128)(2,1)}, u32[]{:S(2)}, u32[]{:S(2)}) collective-permute-start(bf16[8,16,128,128]{3,2,1,0:T(8,128)(2,1)} %bitcast.24), channel_id=1, source_target_pairs={{0,31},{1,0},{2,1},{3,2},{4,3},{5,4},{6,5},{7,6},{8,7},{9,8},{10,9... | collective-permute-start | bytes 12582920 | tf_op jit(solution)/shard_map/ppermute | solution.py:11
  366.9 49.3 %copy-start.1 = (s32[1,32,4,1]{1,3,2,0:T(1,128)S(1)}, s32[1,32,4,1]{1,3,2,0:T(1,128)}, u32[]{:S(2)}) copy-start(s32[1,32,4,1]{1,3,2,0:T(1,128)} %param.9) | copy-start | bytes 1540
  373.3 91.2 %all-to-all-start.1 = ((bf16[8,16,128,128]{3,2,0,1:T(8,128)(2,1)}), bf16[8,16,128,128]{3,2,0,1:T(8,128)(2,1)}, u32[]{:S(2)}, u32[]{:S(2)}) async-start(bf16[8,16,128,128]{3,2,0,1:T(8,128)(2,1)} %bitcast.102), calls=%async_computation.1 | async-start | bytes 8388608 | tf_op jit(solution)/shard_map/all_to_all | solution.py:81
where the time goes:
time: 627 us; the launch traced here: 626 us
  blocking collectives  196 us (31%)
  local copies, waits for them, and re-layouts  182 us (29%)
  matrix products  89.8 us (14%)
  waiting for transfers between devices  85.1 us (14%)
  starting transfers between devices  48.2 us (8%)
  other arithmetic  24.5 us (4%)
    gather x8, local copies, waits for them, and re-layouts, per_group(): picked = flat_table[pick_rows]  148 us
    all_to_all x1, blocking collectives, per_device(): lax.all_to_all(buckets, 'row', split_axis=0, concat_axis=0, tiled=True)  143 us
    dot_general x8, matrix products, per_group(): jnp.einsum('gtab,gstbc->gsac', left_rows, picked, preferred_element_type=...  89.8 us
    all_to_all x1, blocking collectives, per_device(): lax.all_to_all(blocks, 'col', split_axis=0, concat_axis=1, tiled=True)  52.7 us
    all_to_all x1, waiting for transfers between devices, per_device(): lax.all_to_all(result_rows, 'col', split_axis=1, concat_axis=0, tiled=True)  47.3 us
    all_to_all x1, starting transfers between devices, per_device(): lax.all_to_all(result_rows, 'col', split_axis=1, concat_axis=0, tiled=True)  42.9 us
    ppermute x2, waiting for transfers between devices, passed_along(): lax.ppermute(shard, axis, [(i, (i + by) % devices) for i in range(devices)])  37.8 us
  transfers between devices with their start and end apart: 3, of which 2 were waited for; matrix products, arithmetic and copies ran while one was open for 2% of the time, Pallas kernels for 0%

commit v1 on v0

v1 whole, which is shorter than its diff:
```python
import functools
import math

import jax
import jax.numpy as jnp
from jax import lax
from jax.experimental import pallas as pl
from jax.experimental.pallas import tpu as pltpu
from jax.sharding import PartitionSpec as P


def passed_along(shard, axis, by):
    devices = lax.axis_size(axis)
    return lax.ppermute(shard, axis, [(i, (i + by) % devices) for i in range(devices)])


def window_tables(pattern, start_row, row_count, margin, flat_of, empty):
    nblk, slot_count = pattern.shape
    size = row_count + 2 * margin
    ids = (start_row - margin + jnp.arange(size, dtype=jnp.int32) + nblk) % nblk
    cols = pattern[ids]
    match = cols[:, None, :] == ids[None, :, None]
    flat = jnp.asarray(flat_of, jnp.int32)
    place = jnp.where(
        jnp.any(match, axis=-1), jnp.sum(jnp.where(match, flat[:, None, :], 0), axis=-1), empty
    )
    own = cols[margin : margin + row_count]
    column = (own - start_row + margin + nblk) % nblk
    return place.reshape(-1).astype(jnp.int32), column.reshape(-1).astype(jnp.int32)


def fill_dense(place_ref, held, dense, size, tile):
    def fill_row(w, carry):
        rows = pl.ds(pl.multiple_of(w * tile, tile), tile)
        for c in range(size):
            dense[rows, c * tile : (c + 1) * tile] = held[place_ref[w * size + c]]
        return carry

    lax.fori_loop(0, size, fill_row, 0)


def purify(place_ref, column_ref, dense, squared, final, put, dims):
    row_count, slot_count, reach, margin, tile, empty = dims
    size = row_count + 2 * margin
    group = math.gcd(row_count, 4)
    width = group + 2 * reach
    wide = 2 if width % 2 == 0 else 1
    tiles = width // wide

    def per_group(g, carry):
        first = g * group
        low = margin - reach + first

        def cols_of(lo, hi):
            return pl.ds(pl.multiple_of((low + lo) * tile, tile), (hi - lo) * tile)

        own_rows = pl.ds(pl.multiple_of((margin + first) * tile, tile), group * tile)
        spans = []
        for n in range(tiles):
            klo = max(0, n * wide - reach)
            khi = min(width, (n + 1) * wide + reach)
            spans.append((klo, khi))
        for n, (klo, khi) in enumerate(spans):
            product = jnp.dot(
                dense[own_rows, cols_of(klo, khi)],
                dense[cols_of(klo, khi), cols_of(n * wide, (n + 1) * wide)],
                preferred_element_type=jnp.float32,
            )
            for i in range(group):
                for j in range(wide):
                    at = (margin + first + i) * size + low + n * wide + j
                    kept = (place_ref[at] != empty).astype(jnp.float32)
                    part = product[i * tile : (i + 1) * tile, j * tile : (j + 1) * tile] * kept
                    c = n * wide + j
                    squared[i * tile : (i + 1) * tile, c * tile : (c + 1) * tile] = part.astype(
                        squared.dtype
                    )
        for n, (klo, khi) in enumerate(spans):
            cube = jnp.dot(
                squared[:, klo * tile : khi * tile],
                dense[cols_of(klo, khi), cols_of(n * wide, (n + 1) * wide)],
                preferred_element_type=jnp.float32,
            )
            own = squared[:, n * wide * tile : (n + 1) * wide * tile].astype(jnp.float32)
            value = (3.0 * own - 2.0 * cube).astype(final.dtype)
            for j in range(wide):
                final[n * wide + j] = value[:, j * tile : (j + 1) * tile]
        for i in range(group):
            for s in range(slot_count):
                c = column_ref[(first + i) * slot_count + s] - low
                put(first + i, s, final[c, i * tile : (i + 1) * tile, :])
        return carry

    lax.fori_loop(0, row_count // group, per_group, 0)


def local_kernel(dims, place_ref, column_ref, held, out_ref, dense, squared, final):
    row_count, slot_count, reach, margin, tile, empty = dims
    fill_dense(place_ref, held, dense, row_count + 2 * margin, tile)

    def put(i, s, value):
        out_ref[i, s] = value

    purify(place_ref, column_ref, dense, squared, final, put, dims)


def per_device(blocks, pattern, owners):
    row_count, slot_share, tile_size = (blocks.shape[0], blocks.shape[1], blocks.shape[-1])
    slot_count = pattern.shape[1]
    reach = slot_count // 2
    row_pos = lax.axis_index("row")
    col_pos = lax.axis_index("col")
    row_devices = lax.axis_size("row")
    col_devices = lax.axis_size("col")
    row_blocks = lax.all_to_all(blocks, "col", split_axis=0, concat_axis=1, tiled=True)
    local_rows = row_blocks.shape[0]
    hop_count = -(-reach // local_rows)
    lower_list = []
    upper_list = []
    for distance in range(1, hop_count + 1):
        lower_list.append(passed_along(row_blocks, ("row", "col"), distance))
        upper_list.append(passed_along(row_blocks, ("row", "col"), -distance))
    margin = hop_count * local_rows
    size = local_rows + 2 * margin
    empty = size * slot_count
    held = jnp.concatenate(
        [
            part.reshape(-1, tile_size, tile_size)
            for part in lower_list[::-1] + [row_blocks] + upper_list
        ]
        + [jnp.zeros((1, tile_size, tile_size), blocks.dtype)],
        axis=0,
    )
    start_row = (row_pos * col_devices + col_pos) * local_rows
    flat_of = [[w * slot_count + t for t in range(slot_count)] for w in range(size)]
    place, column = window_tables(pattern, start_row, local_rows, margin, flat_of, empty)
    dims = (local_rows, slot_count, reach, margin, tile_size, empty)
    group = math.gcd(local_rows, 4)
    width = group + 2 * reach
    vmem = pl.BlockSpec(memory_space=pltpu.VMEM)
    smem = pl.BlockSpec(memory_space=pltpu.SMEM)
    result_rows = pl.pallas_call(
        functools.partial(local_kernel, dims),
        out_shape=jax.ShapeDtypeStruct(row_blocks.shape, jnp.bfloat16),
        in_specs=[smem, smem, vmem],
        out_specs=vmem,
        scratch_shapes=[
            pltpu.VMEM((size * tile_size, size * tile_size), jnp.bfloat16),
            pltpu.VMEM((group * tile_size, width * tile_size), jnp.bfloat16),
            pltpu.VMEM((width, group * tile_size, tile_size), jnp.bfloat16),
        ],
        compiler_params=pltpu.CompilerParams(vmem_limit_bytes=56 * 2**20),
    )(place, column, held)
    result = lax.all_to_all(result_rows, "col", split_axis=1, concat_axis=0, tiled=True)
    block_count = row_count * slot_share
    capacity = 3 * block_count // (2 * row_devices)
    flat_result = result.reshape(block_count, tile_size, tile_size)
    destination = owners.reshape(block_count)
    one_hot = (destination[:, None] == jnp.arange(row_devices, dtype=jnp.int32)[None, :]).astype(
        jnp.int32
    )
    bucket_rank = jnp.sum((jnp.cumsum(one_hot, axis=0) - 1) * one_hot, axis=1)
    bucket_slot = destination * capacity + bucket_rank
    wanted = jnp.arange(row_devices * capacity, dtype=jnp.int32)
    slot_match = bucket_slot[None, :] == wanted[:, None]
    has_source = jnp.any(slot_match, axis=1)
    source = jnp.sum(
        slot_match.astype(jnp.int32) * jnp.arange(block_count, dtype=jnp.int32)[None, :], axis=1
    )
    padded = jnp.concatenate(
        [flat_result, jnp.zeros((1, tile_size, tile_size), flat_result.dtype)], axis=0
    )
    buckets = padded[jnp.where(has_source, source, block_count)].reshape(
        row_devices, capacity, tile_size, tile_size
    )
    received = lax.all_to_all(buckets, "row", split_axis=0, concat_axis=0, tiled=True)
    return received.reshape(1, 1, row_devices * capacity, tile_size, tile_size)


def solution(mesh):
    in_specs = (P("row", "col", None, None), P(), P("col", "row", None, None))
    out_specs = P("col", "row", None, None, None)
    return jax.shard_map(
        per_device, mesh=mesh, in_specs=in_specs, out_specs=out_specs, check_vma=False
    )
```

time: 627 us -> 409 us (0.65)
  local copies, waits for them, and re-layouts: 182 us -> 27.5 us
  matrix products: 89.8 us -> 0 us
  Pallas kernels: 0 us -> 31.5 us
  other arithmetic: 24.5 us -> 13.8 us
  waiting for transfers between devices: 85.1 us -> 91.5 us
    gather x9 -> x1, local copies, waits for them, and re-layouts: 148 us -> 0.57 us  [window_tables(): cols = pattern[ids]]
    dot_general x8 -> x0, matrix products: 89.8 us -> none  [per_group(): jnp.einsum('gtab,gstbc->gsac', left_rows, picked, preferred_element_type=...]
    pallas_call x0 -> x1, Pallas kernels: none -> 31.5 us  [per_device(): pl.pallas_call(functools.partial(local_kernel, dims), out_shape=jax.Shape...]
    another operation x2 -> x0, other arithmetic: 8.73 us -> none
    another operation x1 -> x0, local copies, waits for them, and re-layouts: 6.42 us -> none
    ppermute x2, waiting for transfers between devices: 37.8 us -> 44.2 us  [passed_along(): lax.ppermute(shard, axis, [(i, (i + by) % devices) for i in range(devices)])]
  transfers between devices with their start and end apart: 3 -> 3, of which waited for: 2 -> 2; matrix products, arithmetic and copies ran while one was open for 2% -> 1% of each run, Pallas kernels for 0% -> 0%
where the time goes in v1:
time: 409 us
  blocking collectives  196 us (48%)
  waiting for transfers between devices  91.5 us (22%)
  starting transfers between devices  48.3 us (12%)
  Pallas kernels  31.5 us (8%)
  local copies, waits for them, and re-layouts  27.5 us (7%)
  other arithmetic  13.8 us (3%)
    all_to_all x1, blocking collectives, per_device(): lax.all_to_all(buckets, 'row', split_axis=0, concat_axis=0, tiled=True)  143 us
    all_to_all x1, blocking collectives, per_device(): lax.all_to_all(blocks, 'col', split_axis=0, concat_axis=1, tiled=True)  52.6 us
    all_to_all x1, waiting for transfers between devices, per_device(): lax.all_to_all(result_rows, 'col', split_axis=1, concat_axis=0, tiled=True)  47.3 us
    ppermute x2, waiting for transfers between devices, passed_along(): lax.ppermute(shard, axis, [(i, (i + by) % devices) for i in range(devices)])  44.2 us
    all_to_all x1, starting transfers between devices, per_device(): lax.all_to_all(result_rows, 'col', split_axis=1, concat_axis=0, tiled=True)  43 us
    pallas_call x1, Pallas kernels, per_device(): pl.pallas_call(functools.partial(local_kernel, dims), out_shape=jax.Shape...  31.5 us
    concatenate x1, other arithmetic, per_device(): jnp.concatenate([part.reshape(-1, tile_size, tile_size) for part in lower...  12.8 us
    gather x1, local copies, waits for them, and re-layouts, per_device(): padded[jnp.where(has_source, source, block_count)]  10.2 us
  transfers between devices with their start and end apart: 3, of which 2 were waited for; matrix products, arithmetic and copies ran while one was open for 1% of the time, Pallas kernels for 0%

profile of v1, /device:TPU:0, one launch (start us, length us, event | category | flops | bytes accessed | tf_op | source)
XLA Modules:
  0.0 408.6 jit_solution(9048039493717125771)
XLA Ops:
  0.0 52.6 %all_to_all.38 = bf16[32,4,128,128]{3,2,1,0:T(8,128)(2,1)S(1)} all-to-all(bf16[32,4,128,128]{3,2,1,0:T(8,128)(2,1)} %param.4), channel_id=1, replica_groups=mesh['row'=8,'col'=4] {'col'}, dimensions={0} | all-to-all | bytes 8388608 | tf_op jit(solution)/shard_map/all_to_all | solution.py:115
  52.6 2.3 copy.23
  54.9 5.3 %collective-permute-start.1 = (bf16[8,16,128,128]{3,2,1,0:T(8,128)(2,1)}, bf16[8,16,128,128]{3,2,1,0:T(8,128)(2,1)}, u32[]{:S(2)}, u32[]{:S(2)}) collective-permute-start(bf16[8,16,128,128]{3,2,1,0:T(8,128)(2,1)} %bitcast.3), channel_id=1, source_target_pairs={{0,31},{1,0},{2,1},{3,2},{4,3},{5,4},{6,5},{7,6},{8,7},{9,8},{10,9... | collective-permute-start | bytes 12582920 | tf_op jit(solution)/shard_map/ppermute | solution.py:14
  60.4 0.6 gather_fusion
  61.0 0.1 compare_reduce_fusion
  61.1 0.2 fusion
  61.3 0.7 select_n.77.place_ref
  62.0 0.7 reshape.132.column_ref
  62.7 44.2 %collective-permute-done = bf16[8,16,128,128]{3,2,1,0:T(8,128)(2,1)} collective-permute-done((bf16[8,16,128,128]{3,2,1,0:T(8,128)(2,1)}, bf16[8,16,128,128]{3,2,1,0:T(8,128)(2,1)}, u32[]{:S(2)}, u32[]{:S(2)}) %collective-permute-start) | collective-permute-done | bytes 4194336 | tf_op jit(solution)/shard_map/ppermute | solution.py:14
  106.8 12.8 %maximum_maximum_fusion.held = bf16[385,128,128]{2,1,0:T(8,128)(2,1)} fusion(bf16[128,128,128]{2,1,0:T(8,128)(2,1)} %bitcast.7, bf16[128,128,128]{2,1,0:T(8,128)(2,1)} %bitcast.5, bf16[128,128,128]{2,1,0:T(8,128)(2,1)} %bitcast.4, bf16[385]{0:T(512)(128)(2,1)S(1)} %pad.4.clone), kind=kLoop, calls=%fused_computation.2 | loop fusion | flops 18923520 | bytes 25199362 | tf_op jit(solution)/shard_map/concatenate | solution.py:126
  119.6 31.5 %shard_map.46 = bf16[8,16,128,128]{3,2,1,0:T(8,128)(2,1)} custom-call(s32[576]{0:T(1024)} %select_n.77.place_ref, s32[128]{0:T(128)} %reshape.132.column_ref, bf16[385,128,128]{2,1,0:T(8,128)(2,1)} %maximum_maximum_fusion.held), custom_call_target="tpu_custom_call" | custom-call | tf_op jit(solution)/shard_map/pallas_call | solution.py:142
  151.1 4.7 %copy.24 = bf16[8,16,128,128]{3,2,0,1:T(8,128)(2,1)} copy(bf16[8,16,128,128]{3,2,1,0:T(8,128)(2,1)} %shard_map.46) | data formatting | bytes 8388608 | tf_op jit(solution)/shard_map/pallas_call | solution.py:142
  155.9 43.0 %all-to-all-start.1 = ((bf16[8,16,128,128]{3,2,0,1:T(8,128)(2,1)}), bf16[8,16,128,128]{3,2,0,1:T(8,128)(2,1)}, u32[]{:S(2)}, u32[]{:S(2)}) async-start(bf16[8,16,128,128]{3,2,0,1:T(8,128)(2,1)} %copy.24), calls=%async_computation.1 | async-start | bytes 8388608 | tf_op jit(solution)/shard_map/all_to_all | solution.py:154
  198.9 0.1 reshape.137
  199.1 0.2 reduce_window_sum.11
  199.3 0.2 select_reduce_fusion.1
  199.5 0.1 fusion.1
  199.6 0.1 select_reduce_fusion
  199.8 47.3 %all-to-all-done.1 = bf16[8,16,128,128]{3,2,0,1:T(8,128)(2,1)} async-done(((bf16[8,16,128,128]{3,2,0,1:T(8,128)(2,1)}), bf16[8,16,128,128]{3,2,0,1:T(8,128)(2,1)}, u32[]{:S(2)}, u32[]{:S(2)}) %all-to-all-start.1) | async-done | bytes 4194336 | tf_op jit(solution)/shard_map/all_to_all | solution.py:154
  247.1 2.5 copy.26
  249.6 2.8 concatenate.7
  252.4 10.2 %gather_fusion.1 = bf16[192,128,128]{2,1,0:T(8,128)(2,1)} fusion(bf16[129,128,128]{2,1,0:T(8,128)(2,1)} %concatenate.7, s32[1024]{0:T(1024)S(1)} %pad_clamp_fusion), kind=kCustom, calls=%fused_computation.1 | custom fusion | bytes 12583680 | tf_op jit(solution)/shard_map/gather | solution.py:173
  262.6 143.2 %all_to_all.39 = bf16[8,24,128,128]{3,2,1,0:T(8,128)(2,1)S(1)} all-to-all(bf16[8,24,128,128]{3,2,1,0:T(8,128)(2,1)} %bitcast.23), channel_id=1, replica_groups=mesh['row'=8,'col'=4] {'row'}, dimensions={0} | all-to-all | bytes 12582912 | tf_op jit(solution)/shard_map/all_to_all | solution.py:176
  405.8 2.7 copy.30
  (21 shorter events, 0.4 us)
Async XLA Ops:
  52.6 7.7 %copy-start = (s32[256,16]{0,1:T(8,128)S(1)}, s32[256,16]{0,1:T(8,128)}, u32[]{:S(2)}) copy-start(s32[256,16]{0,1:T(8,128)} %param.5) | copy-start | bytes 49156
  52.6 8.5 %copy-start.1 = (s32[24,16]{1,0:T(8,128)S(1)}, s32[24,16]{1,0:T(8,128)}, u32[]{:S(2)}) copy-start(s32[24,16]{1,0:T(8,128)} %constant.70.clone) | copy-start | bytes 4612
  54.9 51.9 %collective-permute-start = (bf16[8,16,128,128]{3,2,1,0:T(8,128)(2,1)}, bf16[8,16,128,128]{3,2,1,0:T(8,128)(2,1)}, u32[]{:S(2)}, u32[]{:S(2)}) collective-permute-start(bf16[8,16,128,128]{3,2,1,0:T(8,128)(2,1)} %bitcast.3), channel_id=1, source_target_pairs={{0,1},{1,2},{2,3},{3,4},{4,5},{5,6},{6,7},{7,8},{8,9},{9,10},{10,1... | collective-permute-start | bytes 12582920 | tf_op jit(solution)/shard_map/ppermute | solution.py:14
  54.9 51.9 %collective-permute-start.1 = (bf16[8,16,128,128]{3,2,1,0:T(8,128)(2,1)}, bf16[8,16,128,128]{3,2,1,0:T(8,128)(2,1)}, u32[]{:S(2)}, u32[]{:S(2)}) collective-permute-start(bf16[8,16,128,128]{3,2,1,0:T(8,128)(2,1)} %bitcast.3), channel_id=1, source_target_pairs={{0,31},{1,0},{2,1},{3,2},{4,3},{5,4},{6,5},{7,6},{8,7},{9,8},{10,9... | collective-permute-start | bytes 12582920 | tf_op jit(solution)/shard_map/ppermute | solution.py:14
  155.9 43.0 %copy-start.2 = (s32[1,32,4,1]{1,3,2,0:T(1,128)S(1)}, s32[1,32,4,1]{1,3,2,0:T(1,128)}, u32[]{:S(2)}) copy-start(s32[1,32,4,1]{1,3,2,0:T(1,128)} %param.6) | copy-start | bytes 1540
  155.9 91.2 %all-to-all-start.1 = ((bf16[8,16,128,128]{3,2,0,1:T(8,128)(2,1)}), bf16[8,16,128,128]{3,2,0,1:T(8,128)(2,1)}, u32[]{:S(2)}, u32[]{:S(2)}) async-start(bf16[8,16,128,128]{3,2,0,1:T(8,128)(2,1)} %copy.24), calls=%async_computation.1 | async-start | bytes 8388608 | tf_op jit(solution)/shard_map/all_to_all | solution.py:154
